TPU v7x, 256 devices: a whole 4x4x8 slice. The times are simulated.
256 devices in a mesh: dp: 16 (over y_lo, z), tensor: 16 (over y_hi, x, core).
Axes of the slice: x: 4, y: 4 (y_hi: 2, y_lo: 2; y = y_hi * 2 + y_lo), z: 8, core: 2. Of those that a mesh axis runs over, the one named last changes fastest.
Arguments:
- out_grad: bfloat16 [32768, 4096], P(('dp', 'tensor')), may hold values from -24 to 24
- attn_out: bfloat16 [32768, 4096], P('dp', 'tensor'), may hold values from -0.078125 to 0.078125
- o_weight: bfloat16 [4096, 4096], P('dp', 'tensor'), may hold values from -0.09375 to 0.09375
Outputs:
- attn_grad: bfloat16 [32768, 4096], P('dp', 'tensor')
- weight_grad: float32 [4096, 4096], P('dp', 'tensor')
All inputs are finite; a program needn't handle non-finite values.
Results may differ from a plain program's by a relative error of at most 0.001.
Values may be sent and summed in bfloat16 or wider, within the bound.
No kernel may reach another device: no remote copies, remote signals or barrier semaphores. Data moves between devices by JAX's collectives and lax.ppermute only.
A program may use at most 64 MiB of HBM per device.

v0:
```python
import jax
import jax.numpy as jnp
from jax import lax
from jax.sharding import PartitionSpec as P


def body(out_grad, attn_out, o_weight):
    full_weight = lax.all_gather(o_weight, "dp", axis=0, tiled=True)
    gathered = lax.all_gather(out_grad, "tensor", axis=0, tiled=True)
    attn_grad = jnp.dot(gathered, full_weight, preferred_element_type=jnp.float32).astype(
        jnp.bfloat16
    )
    weight_grad = lax.psum_scatter(
        lax.dot_general(
            gathered, attn_out, (((0,), (0,)), ((), ())), preferred_element_type=jnp.float32
        ),
        "dp",
        scatter_dimension=0,
        tiled=True,
    )
    return (attn_grad, weight_grad)


def solution(mesh):
    return jax.shard_map(
        body,
        mesh=mesh,
        in_specs=(P(("dp", "tensor"), None), P("dp", "tensor"), P("dp", "tensor")),
        out_specs=(P("dp", "tensor"), P("dp", "tensor")),
        check_vma=False,
    )
```

profile of v0, /device:TPU:2, one launch (start us, length us, event | category | flops | bytes accessed | tf_op | source)
XLA Modules:
  0.0 287.6 jit_solution(3332159857697970733)
XLA Ops:
  7.2 0.0 copy-start
  7.2 0.0 all-gather.3.cloned.1.call-start
  7.2 0.7 all-gather.3.cloned.1.call-update
  7.9 0.0 all-gather.5.cloned.1.call-start
  8.0 0.7 all-gather.5.cloned.1.call-update
  8.7 0.0 reduce-scatter.2.cloned.1.call-start
  8.7 119.1 %all-gather.3.cloned.1.call-done = bf16[2048,4096]{1,0:T(8,128)(2,1)} async-done(((bf16[128,4096]{1,0:T(8,128)(2,1)}), bf16[2048,4096]{1,0:T(8,128)(2,1)}) %all-gather.3.cloned.1.call-update) | async-done | bytes 16777232 | tf_op jit(solution)/shard_map/all_gather | solution.py:9
  127.8 0.0 copy-done
  127.8 10.2 %fusion = f32[4096,256]{1,0:T(8,128)} fusion(bf16[2048,4096]{1,0:T(8,128)(2,1)} %all-gather.3.cloned.1.call-done, bf16[2048,256]{1,0:T(8,128)(2,1)S(1)} %copy-done), kind=kOutput, calls=%fused_computation.1 | convolution fusion | flops 4294967296 | bytes 22020096 | tf_op jit(solution)/shard_map/dot_general | solution.py:14
  138.0 0.0 reduce-scatter.2.cloned.1.call-update
  138.0 62.3 %all-gather.5.cloned.1.call-done = bf16[4096,256]{1,0:T(8,128)(2,1)} async-done(((bf16[256,256]{1,0:T(8,128)(2,1)}), bf16[4096,256]{1,0:T(8,128)(2,1)}) %all-gather.5.cloned.1.call-update) | async-done | bytes 2097168 | tf_op jit(solution)/shard_map/all_gather | solution.py:8
  200.3 12.0 %convolution_convert_fusion = bf16[2048,256]{1,0:T(8,128)(2,1)} fusion(bf16[2048,4096]{1,0:T(8,128)(2,1)} %all-gather.3.cloned.1.call-done, bf16[4096,256]{1,0:T(8,128)(2,1)} %all-gather.5.cloned.1.call-done), kind=kOutput, calls=%fused_computation | convolution fusion | flops 4295491584 | bytes 19922944 | tf_op jit(solution)/shard_map/dot_general | solution.py:10
  212.3 68.8 %reduce-scatter.2.cloned.1.call-done = f32[256,256]{1,0:T(8,128)} async-done(((f32[4096,256]{1,0:T(8,128)}), f32[256,256]{1,0:T(8,128)}) %reduce-scatter.2.cloned.1.call-update) | async-done | bytes 262160 | tf_op jit(solution)/shard_map/reduce_scatter | solution.py:13
Async XLA Ops:
  7.2 120.6 %copy-start = (bf16[2048,256]{1,0:T(8,128)(2,1)S(1)}, bf16[2048,256]{1,0:T(8,128)(2,1)}, u32[]{:S(2)}) copy-start(bf16[2048,256]{1,0:T(8,128)(2,1)} %param.4) | copy-start | bytes 3145732
  7.2 120.6 %all-gather.3.cloned.1.call-start = ((), (), s32[]{:S(2)}) async-start(), calls=%async_computation.1 | async-start | bytes 17825792 | tf_op jit(solution)/shard_map/all_gather | solution.py:9
  7.9 192.4 %all-gather.5.cloned.1.call-start = ((), (), s32[]{:S(2)}) async-start(), calls=%async_computation.2 | async-start | bytes 2228224 | tf_op jit(solution)/shard_map/all_gather | solution.py:8
  8.7 272.4 %reduce-scatter.2.cloned.1.call-start = ((), (), s32[]{:S(2)}) async-start(), calls=%async_computation.3 | async-start | bytes 4456448 | tf_op jit(solution)/shard_map/reduce_scatter | solution.py:13
Sparse Core Ops, SparseCore 0:
  10.7 116.9 all-gather.2
  129.5 70.6 all-gather.4
  203.4 77.6 reduce-scatter.1
where the time goes:
time: 288 us
  waiting for transfers between devices  251 us (87%)
  matrix products  22.3 us (8%)
  between operations  13.8 us (5%)
    all_gather x1, waiting for transfers between devices, body(): gathered = lax.all_gather(out_grad, 'tensor', axis=0, tiled=True)  119 us
    reduce_scatter x1, waiting for transfers between devices, body(): lax.psum_scatter(lax.dot_general(gathered, attn_out, (((0,), (0,)), ((),...  68.8 us
    all_gather x1, waiting for transfers between devices, body(): full_weight = lax.all_gather(o_weight, 'dp', axis=0, tiled=True)  62.3 us
    dot_general x1, matrix products, body(): jnp.dot(gathered, full_weight, preferred_element_type=jnp.float32)  12 us
    dot_general x1, matrix products, body(): lax.dot_general(gathered, attn_out, (((0,), (0,)), ((), ())), preferred_e...  10.2 us
  transfers between devices with their start and end apart: 3, of which 3 were waited for; matrix products, arithmetic and copies ran while one was open for 8% of the time, Pallas kernels for 0%

commit v1 on v0

--- a/solution.py
+++ b/solution.py
@@ -5,7 +5,8 @@
 
 
 def body(out_grad, attn_out, o_weight):
-    full_weight = lax.all_gather(o_weight, "dp", axis=0, tiled=True)
+    outgoing = jnp.stack([o_weight] * lax.axis_size("dp"))
+    full_weight = jnp.concatenate(lax.all_to_all(outgoing, "dp", 0, 0), axis=0)
     gathered = lax.all_gather(out_grad, "tensor", axis=0, tiled=True)
     attn_grad = jnp.dot(gathered, full_weight, preferred_element_type=jnp.float32).astype(
         jnp.bfloat16

time: 288 us -> 258 us (0.90)
  waiting for transfers between devices: 251 us -> 146 us
  blocking collectives: 0 us -> 76.6 us
    all_to_all x0 -> x1, blocking collectives: none -> 76.6 us  [body(): full_weight = jnp.concatenate(lax.all_to_all(outgoing, 'dp', 0, 0), axis=0)]
    all_gather x1 -> x0, waiting for transfers between devices: 62.3 us -> none  [body(): full_weight = lax.all_gather(o_weight, 'dp', axis=0, tiled=True)]
    reduce_scatter x1, waiting for transfers between devices: 68.8 us -> 25.7 us  [body(): lax.psum_scatter(lax.dot_general(gathered, attn_out, (((0,), (0,)), ((),...]
  transfers between devices with their start and end apart: 3 -> 2, of which waited for: 3 -> 2; matrix products, arithmetic and copies ran while one was open for 8% -> 4% of each run, Pallas kernels for 0% -> 0%
where the time goes in v1:
time: 258 us
  waiting for transfers between devices  146 us (57%)
  blocking collectives  76.6 us (30%)
  matrix products  19.5 us (8%)
  between operations  14.1 us (5%)
    all_gather x1, waiting for transfers between devices, body(): gathered = lax.all_gather(out_grad, 'tensor', axis=0, tiled=True)  120 us
    all_to_all x1, blocking collectives, body(): full_weight = jnp.concatenate(lax.all_to_all(outgoing, 'dp', 0, 0), axis=0)  76.6 us
    reduce_scatter x1, waiting for transfers between devices, body(): lax.psum_scatter(lax.dot_general(gathered, attn_out, (((0,), (0,)), ((),...  25.7 us
    dot_general x1, matrix products, body(): lax.dot_general(gathered, attn_out, (((0,), (0,)), ((), ())), preferred_e...  10.2 us
    dot_general x1, matrix products, body(): jnp.dot(gathered, full_weight, preferred_element_type=jnp.float32)  9.3 us
  transfers between devices with their start and end apart: 2, of which 2 were waited for; matrix products, arithmetic and copies ran while one was open for 4% of the time, Pallas kernels for 0%

profile of v1, /device:TPU:2, one launch (start us, length us, event | category | flops | bytes accessed | tf_op | source)
XLA Modules:
  0.0 257.5 jit_solution(2824783509480629953)
XLA Ops:
  7.2 0.0 copy-start
  7.2 0.0 all-gather.2.cloned.1.call-start
  7.2 0.7 all-gather.2.cloned.1.call-update
  7.9 0.0 reduce-scatter.2.cloned.1.call-start
  8.0 119.8 %all-gather.2.cloned.1.call-done = bf16[2048,4096]{1,0:T(8,128)(2,1)} async-done(((bf16[128,4096]{1,0:T(8,128)(2,1)}), bf16[2048,4096]{1,0:T(8,128)(2,1)}) %all-gather.2.cloned.1.call-update) | async-done | bytes 16777232 | tf_op jit(solution)/shard_map/all_gather | solution.py:10
  127.8 0.0 copy-done
  127.8 10.2 %fusion = f32[4096,256]{1,0:T(8,128)} fusion(bf16[2048,4096]{1,0:T(8,128)(2,1)} %all-gather.2.cloned.1.call-done, bf16[2048,256]{1,0:T(8,128)(2,1)S(1)} %copy-done), kind=kOutput, calls=%fused_computation.1 | convolution fusion | flops 4294967296 | bytes 22020096 | tf_op jit(solution)/shard_map/dot_general | solution.py:15
  138.0 0.0 copy-start.1
  138.0 0.0 reduce-scatter.2.cloned.1.call-update
  138.0 0.9 copy-done.1
  138.9 0.2 stack.2
  139.1 76.6 %all_to_all.5 = bf16[16,256,256]{2,1,0:T(8,128)(2,1)S(1)} all-to-all(bf16[16,256,256]{2,1,0:T(8,128)(2,1)S(1)} %stack.2), channel_id=1, replica_groups=mesh['dp'=16,'tensor'=16] {'dp'}, dimensions={0} | all-to-all | bytes 4194304 | tf_op jit(solution)/shard_map/all_to_all | solution.py:9
  215.6 9.3 %convolution_convert_fusion = bf16[2048,256]{1,0:T(8,128)(2,1)} fusion(bf16[2048,4096]{1,0:T(8,128)(2,1)} %all-gather.2.cloned.1.call-done, bf16[4096,256]{1,0:T(8,128)(2,1)S(1)} %bitcast.5), kind=kOutput, calls=%fused_computation | convolution fusion | flops 4295491584 | bytes 19922944 | tf_op jit(solution)/shard_map/dot_general | solution.py:11
  225.0 25.7 %reduce-scatter.2.cloned.1.call-done = f32[256,256]{1,0:T(8,128)} async-done(((f32[4096,256]{1,0:T(8,128)}), f32[256,256]{1,0:T(8,128)}) %reduce-scatter.2.cloned.1.call-update) | async-done | bytes 262160 | tf_op jit(solution)/shard_map/reduce_scatter | solution.py:14
Async XLA Ops:
  7.2 120.6 %copy-start = (bf16[2048,256]{1,0:T(8,128)(2,1)S(1)}, bf16[2048,256]{1,0:T(8,128)(2,1)}, u32[]{:S(2)}) copy-start(bf16[2048,256]{1,0:T(8,128)(2,1)} %param.4) | copy-start | bytes 3145732
  7.2 120.6 %all-gather.2.cloned.1.call-start = ((), (), s32[]{:S(2)}) async-start(), calls=%async_computation.2 | async-start | bytes 17825792 | tf_op jit(solution)/shard_map/all_gather | solution.py:10
  7.9 242.7 %reduce-scatter.2.cloned.1.call-start = ((), (), s32[]{:S(2)}) async-start(), calls=%async_computation.3 | async-start | bytes 4456448 | tf_op jit(solution)/shard_map/reduce_scatter | solution.py:14
  138.0 0.9 copy-start.1
Sparse Core Ops, SparseCore 0:
  10.7 116.9 all-gather.1
  138.1 112.4 reduce-scatter.1
